TPU v7x, 128 devices: a whole 4x4x4 slice. The times are simulated.
128 devices in a mesh: cube: 32 (over z, y, core), band: 4 (over x).
Axes of the slice: x: 4, y: 4, z: 4, core: 2. Of those that a mesh axis runs over, the one named last changes fastest.
Arguments:
- vis: bfloat16 [32, 864, 512], P('cube', 'band'), may hold values from -6 to 6
- keep_slots: int32 [32, 864], P('cube', 'band'), may hold values from 0 to 1727, as said below
- counts: int32 [32, 4], P('cube', 'band'), may hold values from 108 to 216, as said below
- band_mask: int32 [32, 4], P('cube'), may hold values from 0 to 1, as said below
- mask_token: float32 [512], replicated, may hold values from -6 to 6
- pos: bfloat16 [1728, 512], P('band'), may hold values from -3 to 3
- ln1_gain: float32 [512], replicated, may hold values from 0.5 to 1.5
- ln1_bias: float32 [512], replicated, may hold values from -1.8 to 1.8
- w_qkv: bfloat16 [512, 1536], replicated, may hold values from -0.25 to 0.25
- b_query: float32 [512], replicated, may hold values from -3 to 3
- b_value: float32 [512], replicated, may hold values from -3 to 3
- w_out: bfloat16 [512, 512], replicated, may hold values from -2 to 2
- b_out: float32 [512], replicated, may hold values from -1.8 to 1.8
- ln2_gain: float32 [512], replicated, may hold values from 0.5 to 1.5
- ln2_bias: float32 [512], replicated, may hold values from -1.8 to 1.8
- w_up: bfloat16 [512, 2048], replicated, may hold values from -0.25 to 0.25
- b_up: float32 [2048], replicated, may hold values from -1.8 to 1.8
- w_down: bfloat16 [2048, 512], replicated, may hold values from -0.125 to 0.125
- b_down: float32 [512], replicated, may hold values from -1.8 to 1.8
- d_out: bfloat16 [32, 1728, 512], P('cube', 'band'), may hold values from -6 to 6
Outputs:
- out: bfloat16 [32, 1728, 512], P('cube', 'band')
- grad_vis: bfloat16 [32, 864, 512], P('cube', 'band')
- grad_mask_token: float32 [512], replicated
- grad_pos: float32 [1728, 512], P('band')
- grad_ln1_gain: float32 [512], replicated
- grad_ln1_bias: float32 [512], replicated
- grad_w_qkv: float32 [512, 1536], replicated
- grad_b_query: float32 [512], replicated
- grad_b_value: float32 [512], replicated
- grad_w_out: float32 [512, 512], replicated
- grad_b_out: float32 [512], replicated
- grad_ln2_gain: float32 [512], replicated
- grad_ln2_bias: float32 [512], replicated
- grad_w_up: float32 [512, 2048], replicated
- grad_b_up: float32 [2048], replicated
- grad_w_down: float32 [2048, 512], replicated
- grad_b_down: float32 [512], replicated
Inputs may be any that keep to these rules, and one draw needn't show every extreme that they name: `keep_slots`: within a cube the entries are distinct slots; of the rows of one piece, at most 72 name slots of one band group, and some piece with all its rows counted has 72 for some group. `counts`: the value 216 is taken in every draw. `band_mask`: each cube has all groups, or all but one.
All inputs are finite; a program needn't handle non-finite values.
Results may differ from a plain program's by a relative error of at most 0.018.
Values may be sent and summed in bfloat16 or wider, within the bound.
No kernel may reach another device: no remote copies, remote signals or barrier semaphores. Data moves between devices by JAX's collectives and lax.ppermute only.
A program may use at most 128 MiB of HBM per device.

v0:
```python
import jax
import jax.numpy as jnp
from jax import lax
from jax.sharding import PartitionSpec as P

HEADS = 16
CAP = 72


epsilon = 1e-05
neg_large = -1e30


def normalize(values, gain, offset):
    average = jnp.mean(values, axis=-1, keepdims=True)
    centered = values - average
    variance = jnp.mean(centered * centered, axis=-1, keepdims=True)
    return centered * lax.rsqrt(variance + epsilon) * gain + offset


def smooth_gate(values):
    return jax.nn.gelu(values, approximate=True)


def to_heads(tensor, quads):
    cubes, length, width = tensor.shape
    depth = width // (quads * 4)
    split = tensor.reshape(cubes, length, quads, 4, depth)
    return split.transpose(0, 2, 3, 1, 4).reshape(cubes * quads, 4, length, depth)


def from_heads(tensor, cubes):
    items, four, length, depth = tensor.shape
    quads = items // cubes
    shaped = tensor.reshape(cubes, quads, four, length, depth)
    return shaped.transpose(0, 3, 1, 2, 4).reshape(cubes, length, quads * four * depth)


def masked_scores(queries, keys, live):
    scale = queries.shape[-1] ** (-0.5)
    scores = jnp.einsum("hqd,hkd->hqk", queries, keys, preferred_element_type=jnp.float32) * scale
    return (jnp.where(live[None, None, :], scores, neg_large), scale)


def attend_forward(items):
    queries, keys, values, live = items
    scores, scale = masked_scores(queries, keys, live)
    peak = jnp.max(scores, axis=-1, keepdims=True)
    weights = jnp.exp(scores - peak)
    total = jnp.sum(weights, axis=-1, keepdims=True)
    attention = (weights / total).astype(jnp.bfloat16)
    mixed = jnp.einsum("hqk,hkd->hqd", attention, values, preferred_element_type=jnp.float32)
    return (mixed, peak + jnp.log(total))


def score_grads(queries, keys, values, live, log_total, grad_mixed):
    scores, scale = masked_scores(queries, keys, live)
    attention = jnp.exp(scores - log_total)
    grad_attention = jnp.einsum(
        "hqd,hkd->hqk", grad_mixed, values, preferred_element_type=jnp.float32
    )
    inner = jnp.sum(attention * grad_attention, axis=-1, keepdims=True)
    grad_scores = (attention * (grad_attention - inner)).astype(jnp.bfloat16)
    return (attention, grad_scores, inner, scale)


def attend_backward(items):
    queries, keys, values, live, log_total, grad_mixed = items
    attention, grad_scores, inner, scale = score_grads(
        queries, keys, values, live, log_total, grad_mixed
    )
    grad_queries = (
        jnp.einsum("hqk,hkd->hqd", grad_scores, keys, preferred_element_type=jnp.float32) * scale
    )
    grad_keys = (
        jnp.einsum("hqk,hqd->hkd", grad_scores, queries, preferred_element_type=jnp.float32) * scale
    )
    grad_values = jnp.einsum(
        "hqk,hqd->hkd",
        attention.astype(jnp.bfloat16),
        grad_mixed,
        preferred_element_type=jnp.float32,
    )
    return (grad_queries, grad_keys, grad_values)


def token_sum(tensor):
    return jnp.sum(tensor.astype(jnp.float32), axis=(0, 1))


def body(
    vis,
    keep_slots,
    counts,
    band_mask,
    mask_token,
    pos,
    ln1_gain,
    ln1_bias,
    w_qkv,
    b_query,
    b_value,
    w_out,
    b_out,
    ln2_gain,
    ln2_bias,
    w_up,
    b_up,
    w_down,
    b_down,
    d_out,
):
    groups = lax.axis_size("band")
    owner = lax.axis_index("band")
    cubes, piece = keep_slots.shape
    length = pos.shape[0]
    width = vis.shape[2]
    quads = HEADS // 4
    capacity = CAP
    positions = lax.broadcasted_iota(jnp.int32, (cubes, piece), 1)
    slot_ids = jnp.where(positions < counts, keep_slots, -1)
    target = jnp.where(slot_ids >= 0, slot_ids // length, -1)
    group_ids = lax.broadcasted_iota(jnp.int32, (cubes, groups, piece), 1)
    bound_for = (target[:, None, :] == group_ids).astype(jnp.int32)
    ranks = jnp.cumsum(bound_for, axis=2) - 1
    rank_ids = lax.broadcasted_iota(jnp.int32, (cubes, groups, capacity, piece), 2)
    select = (bound_for[:, :, None, :] == 1) & (ranks[:, :, None, :] == rank_ids)
    select_low = select.astype(jnp.bfloat16)
    outgoing = jnp.einsum(
        "cgqr,crd->cgqd", select_low, vis, preferred_element_type=jnp.float32
    ).astype(jnp.bfloat16)
    outgoing_ids = jnp.sum(jnp.where(select, slot_ids[:, None, None, :] + 1, 0), axis=3) - 1
    arrived, arrived_ids = (
        lax.all_to_all(outgoing, "band", split_axis=1, concat_axis=1, tiled=True),
        lax.all_to_all(outgoing_ids, "band", split_axis=1, concat_axis=1, tiled=True),
    )
    arrived = arrived.reshape(cubes, groups * capacity, width)
    arrived_ids = arrived_ids.reshape(cubes, groups * capacity)
    received = arrived_ids.shape[1]
    local_slots = lax.broadcasted_iota(jnp.int32, (cubes, length, received), 1) + owner * length
    placing = arrived_ids[:, None, :] == local_slots
    placing_low = placing.astype(jnp.bfloat16)
    placed = jnp.einsum("csj,cjd->csd", placing_low, arrived, preferred_element_type=jnp.float32)
    visible = jnp.sum(placing.astype(jnp.float32), axis=2, keepdims=True)
    start = placed + (1.0 - visible) * mask_token + pos.astype(jnp.float32)
    normed_first = normalize(start, ln1_gain, ln1_bias).astype(jnp.bfloat16)
    projected = jnp.einsum("csd,de->cse", normed_first, w_qkv, preferred_element_type=jnp.float32)
    queries = (projected[..., :width] + b_query).astype(jnp.bfloat16)
    keys = projected[..., width : 2 * width].astype(jnp.bfloat16)
    values = (projected[..., 2 * width :] + b_value).astype(jnp.bfloat16)
    all_keys, all_values = (
        lax.all_gather(keys, "band", axis=1, tiled=True),
        lax.all_gather(values, "band", axis=1, tiled=True),
    )
    live = jnp.repeat(band_mask > 0, length, axis=1)
    live_items = jnp.repeat(live, quads, axis=0)
    head_query = to_heads(queries, quads)
    head_key = to_heads(all_keys, quads)
    head_value = to_heads(all_values, quads)
    head_mixed, log_total = lax.map(attend_forward, (head_query, head_key, head_value, live_items))
    mixed = from_heads(head_mixed, cubes).astype(jnp.bfloat16)
    branch = jnp.einsum("csd,de->cse", mixed, w_out, preferred_element_type=jnp.float32) + b_out
    middle = start + branch
    normed_second = normalize(middle, ln2_gain, ln2_bias).astype(jnp.bfloat16)
    up_value = (
        jnp.einsum("csd,df->csf", normed_second, w_up, preferred_element_type=jnp.float32) + b_up
    )
    activated = smooth_gate(up_value).astype(jnp.bfloat16)
    result = middle + (
        jnp.einsum("csf,fd->csd", activated, w_down, preferred_element_type=jnp.float32) + b_down
    )
    out = result.astype(jnp.bfloat16)
    grad_result = d_out.astype(jnp.float32)
    grad_b_down = token_sum(grad_result)
    grad_w_down = jnp.einsum("csf,csd->fd", activated, d_out, preferred_element_type=jnp.float32)
    grad_activated = jnp.einsum("csd,fd->csf", d_out, w_down, preferred_element_type=jnp.float32)
    _, gate_pull = jax.vjp(smooth_gate, up_value)
    grad_up = gate_pull(grad_activated)[0].astype(jnp.bfloat16)
    grad_b_up = token_sum(grad_up)
    grad_w_up = jnp.einsum(
        "csd,csf->df", normed_second, grad_up, preferred_element_type=jnp.float32
    )
    grad_second = jnp.einsum("csf,df->csd", grad_up, w_up, preferred_element_type=jnp.float32)
    _, second_pull = jax.vjp(normalize, middle, ln2_gain, ln2_bias)
    grad_middle_part, grad_ln2_gain, grad_ln2_bias = second_pull(grad_second)
    grad_middle = grad_result + grad_middle_part
    grad_branch = grad_middle.astype(jnp.bfloat16)
    grad_b_out = token_sum(grad_branch)
    grad_w_out = jnp.einsum("csd,cse->de", mixed, grad_branch, preferred_element_type=jnp.float32)
    grad_mixed = jnp.einsum(
        "cse,de->csd", grad_branch, w_out, preferred_element_type=jnp.float32
    ).astype(jnp.bfloat16)
    head_grad_mixed = to_heads(grad_mixed, quads)
    grad_query_heads, grad_key_heads, grad_value_heads = lax.map(
        attend_backward, (head_query, head_key, head_value, live_items, log_total, head_grad_mixed)
    )
    grad_queries = from_heads(grad_query_heads, cubes).astype(jnp.bfloat16)
    part_keys = from_heads(grad_key_heads, cubes)
    part_values = from_heads(grad_value_heads, cubes)
    sum_keys, sum_values = (
        lax.psum_scatter(
            part_keys.astype(jnp.bfloat16), "band", scatter_dimension=1, tiled=True
        ).astype(jnp.float32),
        lax.psum_scatter(
            part_values.astype(jnp.bfloat16), "band", scatter_dimension=1, tiled=True
        ).astype(jnp.float32),
    )
    grad_keys = sum_keys.astype(jnp.bfloat16)
    grad_values = sum_values.astype(jnp.bfloat16)
    grad_projected = jnp.concatenate((grad_queries, grad_keys, grad_values), axis=2)
    grad_b_query = token_sum(grad_queries)
    grad_b_value = token_sum(grad_values)
    grad_w_qkv = jnp.einsum(
        "csd,cse->de", normed_first, grad_projected, preferred_element_type=jnp.float32
    )
    grad_first = jnp.einsum(
        "cse,de->csd", grad_projected, w_qkv, preferred_element_type=jnp.float32
    )
    _, first_pull = jax.vjp(normalize, start, ln1_gain, ln1_bias)
    grad_start_part, grad_ln1_gain, grad_ln1_bias = first_pull(grad_first)
    grad_start = grad_middle + grad_start_part
    grad_pos = lax.psum(jnp.sum(grad_start, axis=0).astype(jnp.bfloat16), "cube").astype(
        jnp.float32
    )
    grad_mask_token = jnp.sum((1.0 - visible) * grad_start, axis=(0, 1))
    grad_slots = (visible * grad_start).astype(jnp.bfloat16)
    grad_arrived = jnp.einsum(
        "csj,csd->cjd", placing_low, grad_slots, preferred_element_type=jnp.float32
    )
    returned = lax.all_to_all(
        grad_arrived.astype(jnp.bfloat16).reshape(cubes, groups, capacity, width),
        "band",
        split_axis=1,
        concat_axis=1,
        tiled=True,
    )
    grad_vis = jnp.einsum(
        "cgqr,cgqd->crd", select_low, returned, preferred_element_type=jnp.float32
    ).astype(jnp.bfloat16)
    (
        grad_mask_token,
        grad_ln1_gain,
        grad_ln1_bias,
        grad_w_qkv,
        grad_b_query,
        grad_b_value,
        grad_w_out,
        grad_b_out,
        grad_ln2_gain,
        grad_ln2_bias,
        grad_w_up,
        grad_b_up,
        grad_w_down,
        grad_b_down,
    ) = lax.psum(
        (
            grad_mask_token,
            grad_ln1_gain,
            grad_ln1_bias,
            grad_w_qkv,
            grad_b_query,
            grad_b_value,
            grad_w_out,
            grad_b_out,
            grad_ln2_gain,
            grad_ln2_bias,
            grad_w_up,
            grad_b_up,
            grad_w_down,
            grad_b_down,
        ),
        ("cube", "band"),
    )
    return (
        out,
        grad_vis,
        grad_mask_token,
        grad_pos,
        grad_ln1_gain,
        grad_ln1_bias,
        grad_w_qkv,
        grad_b_query,
        grad_b_value,
        grad_w_out,
        grad_b_out,
        grad_ln2_gain,
        grad_ln2_bias,
        grad_w_up,
        grad_b_up,
        grad_w_down,
        grad_b_down,
    )


def solution(mesh):
    return jax.shard_map(
        body,
        mesh=mesh,
        in_specs=(
            P("cube", "band", None),
            P("cube", "band"),
            P("cube", "band"),
            P("cube", None),
            P(),
            P("band", None),
            P(),
            P(),
            P(),
            P(),
            P(),
            P(),
            P(),
            P(),
            P(),
            P(),
            P(),
            P(),
            P(),
            P("cube", "band", None),
        ),
        out_specs=(
            P("cube", "band", None),
            P("cube", "band", None),
            P(),
            P("band", None),
            P(),
            P(),
            P(),
            P(),
            P(),
            P(),
            P(),
            P(),
            P(),
            P(),
            P(),
            P(),
            P(),
        ),
        check_vma=False,
    )
```

profile of v0, /device:TPU:1, one launch (start us, length us, event | category | flops | bytes accessed | tf_op | source)
XLA Modules:
  0.0 643.7 jit_solution(622730167767224771)
XLA Ops:
  11.2 4.8 all-to-all-start
  40.2 27.0 %all-gather.3.cloned.1.call-done = bf16[1,1728,512]{2,1,0:T(8,128)(2,1)} async-done(((bf16[1,432,512]{2,1,0:T(8,128)(2,1)}), bf16[1,1728,512]{2,1,0:T(8,128)(2,1)}) %all-gather.3.cloned.1.call-update) | async-done | bytes 1769488 | tf_op jit(solution)/shard_map/all_gather | solution.py:152
  67.2 3.7 copy.61
  71.0 26.6 %all-gather.5.cloned.1.call-done = bf16[1,1728,512]{2,1,0:T(8,128)(2,1)} async-done(((bf16[1,432,512]{2,1,0:T(8,128)(2,1)}), bf16[1,1728,512]{2,1,0:T(8,128)(2,1)}) %all-gather.5.cloned.1.call-update) | async-done | bytes 1769488 | tf_op jit(solution)/shard_map/all_gather | solution.py:153
  97.6 3.7 copy.62
  102.2 42.6 %while.26 = (s32[]{:T(128)}, bf16[4,4,432,32]{2,3,1,0:T(8,128)(2,1)}, f32[4,4,432,1]{2,1,3,0:T(4,128)S(1)}, pred[4,1728]{1,0:T(4,128)(4,1)S(1)}, bf16[4,4,432,32...) while((s32[]{:T(128)}, ...), condition=%wide.region_9.10_spmd, body=%wide.region_6.9_spmd.sunk | while | flops 418036032 | bytes 37212772 | solution.py:160
  108.0 4.8 fusion.148
  118.6 4.8 fusion.148
  129.3 4.8 fusion.148
  139.9 4.8 fusion.148
  148.3 3.9 convert_reduce_fusion
  160.2 106.8 %while.27 = (s32[]{:T(128)}, bf16[4,4,432,32]{2,3,1,0:T(8,128)(2,1)}, bf16[4,4,1728,32]{2,3,1,0:T(8,128)(2,1)}, bf16[4,4,1728,32]{2,3,1,0:T(8,128)(2,1)}, pred[4...) while((s32[]{:T(128)}, ...), condition=%wide.region_16.17_spmd, body=%wide.region_14.16_spmd.sunk | while | flops 1000579392 | bytes 126820472 | solution.py:194
  163.1 8.3 %multiply_reduce_fusion.9 = (f32[4,432]{1,0:T(4,128)S(1)}, f32[4,432,1728]{2,1,0:T(8,128)}) fusion(f32[4,432,1728]{2,1,0:T(8,128)S(1)} %fusion.157, f32[4,432]{1,0:T(4,128)S(1)} %dynamic-slice_bitcast_fusion.2, pred[1728]{0:T(1024)(128)(4,1)S(1)} %dynamic-slice_reduce_fusion.5, bf16[4,4,1728,32]{2,3,1,0:T(8,128)(2,1)} %get-tuple-element.360, ...), kind=kOutput, calls=%fused_computation.22.clone.1 | convolution fusion | flops 206031168 | bytes 24938240 | tf_op jit(solution)/shard_map/while/body/eval_jaxpr/hqd,hkd->hqk/dot_general | solution.py:59
  171.4 6.7 %multiply_convert_fusion.6 = bf16[4,432,1728]{2,1,0:T(8,128)(2,1)S(1)} fusion(f32[4,432,1728]{2,1,0:T(8,128)} %get-tuple-element.303, f32[4,432,1728]{2,1,0:T(8,128)S(1)} %fusion.157, f32[4,432]{1,0:T(4,128)S(1)} %get-tuple-element.304, f32[4,432]{1,0:T(4,128)S(1)} %dynamic-slice_bitcast_fusion.2, pred[1728]{0:T(1024)(128)(4,1)S(1)} %dynamic-slice_reduce_fusion.5), kind=kLoop, calls=%fused_computation.21.clone.1 | loop fusion | flops 17915904 | bytes 29875392 | tf_op jit(solution)/shard_map/while/body/eval_jaxpr/convert_element_type | solution.py:63
  189.8 8.3 %multiply_reduce_fusion.9 = (f32[4,432]{1,0:T(4,128)S(1)}, f32[4,432,1728]{2,1,0:T(8,128)}) fusion(f32[4,432,1728]{2,1,0:T(8,128)S(1)} %fusion.157, f32[4,432]{1,0:T(4,128)S(1)} %dynamic-slice_bitcast_fusion.2, pred[1728]{0:T(1024)(128)(4,1)S(1)} %dynamic-slice_reduce_fusion.5, bf16[4,4,1728,32]{2,3,1,0:T(8,128)(2,1)} %get-tuple-element.360, ...), kind=kOutput, calls=%fused_computation.22.clone.1 | convolution fusion | flops 206031168 | bytes 24938240 | tf_op jit(solution)/shard_map/while/body/eval_jaxpr/hqd,hkd->hqk/dot_general | solution.py:59
  198.1 6.7 %multiply_convert_fusion.6 = bf16[4,432,1728]{2,1,0:T(8,128)(2,1)S(1)} fusion(f32[4,432,1728]{2,1,0:T(8,128)} %get-tuple-element.303, f32[4,432,1728]{2,1,0:T(8,128)S(1)} %fusion.157, f32[4,432]{1,0:T(4,128)S(1)} %get-tuple-element.304, f32[4,432]{1,0:T(4,128)S(1)} %dynamic-slice_bitcast_fusion.2, pred[1728]{0:T(1024)(128)(4,1)S(1)} %dynamic-slice_reduce_fusion.5), kind=kLoop, calls=%fused_computation.21.clone.1 | loop fusion | flops 17915904 | bytes 29875392 | tf_op jit(solution)/shard_map/while/body/eval_jaxpr/convert_element_type | solution.py:63
  216.5 8.3 %multiply_reduce_fusion.9 = (f32[4,432]{1,0:T(4,128)S(1)}, f32[4,432,1728]{2,1,0:T(8,128)}) fusion(f32[4,432,1728]{2,1,0:T(8,128)S(1)} %fusion.157, f32[4,432]{1,0:T(4,128)S(1)} %dynamic-slice_bitcast_fusion.2, pred[1728]{0:T(1024)(128)(4,1)S(1)} %dynamic-slice_reduce_fusion.5, bf16[4,4,1728,32]{2,3,1,0:T(8,128)(2,1)} %get-tuple-element.360, ...), kind=kOutput, calls=%fused_computation.22.clone.1 | convolution fusion | flops 206031168 | bytes 24938240 | tf_op jit(solution)/shard_map/while/body/eval_jaxpr/hqd,hkd->hqk/dot_general | solution.py:59
  224.8 6.7 %multiply_convert_fusion.6 = bf16[4,432,1728]{2,1,0:T(8,128)(2,1)S(1)} fusion(f32[4,432,1728]{2,1,0:T(8,128)} %get-tuple-element.303, f32[4,432,1728]{2,1,0:T(8,128)S(1)} %fusion.157, f32[4,432]{1,0:T(4,128)S(1)} %get-tuple-element.304, f32[4,432]{1,0:T(4,128)S(1)} %dynamic-slice_bitcast_fusion.2, pred[1728]{0:T(1024)(128)(4,1)S(1)} %dynamic-slice_reduce_fusion.5), kind=kLoop, calls=%fused_computation.21.clone.1 | loop fusion | flops 17915904 | bytes 29875392 | tf_op jit(solution)/shard_map/while/body/eval_jaxpr/convert_element_type | solution.py:63
  243.2 8.3 %multiply_reduce_fusion.9 = (f32[4,432]{1,0:T(4,128)S(1)}, f32[4,432,1728]{2,1,0:T(8,128)}) fusion(f32[4,432,1728]{2,1,0:T(8,128)S(1)} %fusion.157, f32[4,432]{1,0:T(4,128)S(1)} %dynamic-slice_bitcast_fusion.2, pred[1728]{0:T(1024)(128)(4,1)S(1)} %dynamic-slice_reduce_fusion.5, bf16[4,4,1728,32]{2,3,1,0:T(8,128)(2,1)} %get-tuple-element.360, ...), kind=kOutput, calls=%fused_computation.22.clone.1 | convolution fusion | flops 206031168 | bytes 24938240 | tf_op jit(solution)/shard_map/while/body/eval_jaxpr/hqd,hkd->hqk/dot_general | solution.py:59
  251.5 6.7 %multiply_convert_fusion.6 = bf16[4,432,1728]{2,1,0:T(8,128)(2,1)S(1)} fusion(f32[4,432,1728]{2,1,0:T(8,128)} %get-tuple-element.303, f32[4,432,1728]{2,1,0:T(8,128)S(1)} %fusion.157, f32[4,432]{1,0:T(4,128)S(1)} %get-tuple-element.304, f32[4,432]{1,0:T(4,128)S(1)} %dynamic-slice_bitcast_fusion.2, pred[1728]{0:T(1024)(128)(4,1)S(1)} %dynamic-slice_reduce_fusion.5), kind=kLoop, calls=%fused_computation.21.clone.1 | loop fusion | flops 17915904 | bytes 29875392 | tf_op jit(solution)/shard_map/while/body/eval_jaxpr/convert_element_type | solution.py:63
  267.0 8.7 %copy.67 = bf16[1,1728,512]{2,0,1:T(2,128)(2,1)} copy(bf16[1,1728,512]{1,2,0:T(8,128)(2,1)} %bitcast.253) | data formatting | bytes 3538944
  279.5 8.7 %copy.65 = bf16[1,1728,512]{2,0,1:T(2,128)(2,1)} copy(bf16[1,1728,512]{1,2,0:T(8,128)(2,1)} %bitcast.252) | data formatting | bytes 3538944
  288.3 3.8 copy.74
  294.9 5.1 fusion.107
  300.0 3.7 fusion.80
  312.4 23.4 %reduce-scatter.7.cloned.1.call-done = bf16[432,512]{1,0:T(8,128)(2,1)} async-done(((bf16[1728,512]{1,0:T(8,128)(2,1)}), bf16[432,512]{1,0:T(8,128)(2,1)}) %reduce-scatter.7.cloned.1.call-update) | async-done | bytes 442384
  347.0 4.4 fusion.72
  351.7 4.3 fusion.64
  362.3 67.6 %all-reduce.1 = (f32[512]{0:T(512)}, f32[512]{0:T(512)}, f32[512]{0:T(512)}, f32[512]{0:T(512)}, f32[512]{0:T(512)}, /*index=5*/f32[512]{0:T(512)}, f32[512]{0:T...) all-reduce(f32[512]{0:T(512)S(1)} %multiply_reduce_fusion.3, ...), channel_id=1, replica_groups=mesh['cube'=32,'band'=4] {'cube','band'}, use_global_device_ids=true, to_apply=%region_22.23 | all-reduce | flops 6656 | bytes 53248 | tf_op jit(solution)/shard_map/psum | solution.py:255
  429.9 19.8 %all-reduce.6.cloned.1.call-done = bf16[432,512]{1,0:T(8,128)(2,1)} async-done(((bf16[432,512]{1,0:T(8,128)(2,1)}), bf16[432,512]{1,0:T(8,128)(2,1)}) %all-reduce.6.cloned.1.call-update) | async-done | bytes 442384 | tf_op jit(solution)/shard_map/psum | solution.py:222
  452.7 173.1 %all-reduce.8.cloned.1.call-done = (f32[512,1536]{1,0:T(8,128)}, f32[512,512]{1,0:T(8,128)}, f32[512,2048]{1,0:T(8,128)}, f32[2048,512]{1,0:T(8,128)}) async-done(((f32[512,1536]{1,0:T(8,128)}, f32[512,512]{1,0:T(8,128)}, f32[512,2048]{1,0:T(8,128)}, f32[2048,512]{1,0:T(8,128)}), (f32[512,1536]{1,0:T(8,128)}, f32[512,512]{1,0:T(8,128)}, f32[512,2048]{1,0:T(8,128)}, ...) | async-done | bytes 12582928 | tf_op jit(solution)/shard_map/psum | solution.py:255
  625.8 3.9 copy.109
  (312 shorter events, 151.4 us)
Async XLA Ops:
  7.2 141.0 %copy-start = (bf16[2048,512]{1,0:T(8,128)(2,1)S(1)}, bf16[2048,512]{1,0:T(8,128)(2,1)}, u32[]{:S(2)}) copy-start(bf16[2048,512]{1,0:T(8,128)(2,1)} %param.41) | copy-start | bytes 6291460
  7.2 23.9 %copy-start.69 = (f32[512]{0:T(512)S(1)}, f32[512]{0:T(512)}, u32[]{:S(2)}) copy-start(f32[512]{0:T(512)} %param.31) | copy-start | bytes 6148
  7.2 23.9 %copy-start.60 = (f32[512]{0:T(512)S(1)}, f32[512]{0:T(512)}, u32[]{:S(2)}) copy-start(f32[512]{0:T(512)} %param.30) | copy-start | bytes 6148
  10.1 10.0 %copy-start.52 = (pred[4,216]{1,0:T(4,128)(4,1)}, pred[4,216]{1,0:T(4,128)(4,1)S(1)}, u32[]{:S(2)}) copy-start(pred[4,216]{1,0:T(4,128)(4,1)S(1)} %convert_compare_fusion) | copy-start | bytes 2596
  10.4 9.6 %copy-start.38 = (s32[4,216]{1,0:T(4,128)}, s32[4,216]{1,0:T(4,128)S(1)}, u32[]{:S(2)}) copy-start(s32[4,216]{1,0:T(4,128)S(1)} %fusion.102) | copy-start | bytes 10372
  11.2 8.9 %all-to-all-start = ((s32[1,4,72]{2,0,1:T(1,128)}), s32[1,4,72]{2,0,1:T(1,128)S(1)}, u32[]{:S(2)}, u32[]{:S(2)}) async-start(s32[1,4,72]{2,0,1:T(1,128)} %bitcast.19), calls=%async_computation | async-start | bytes 4096 | tf_op jit(solution)/shard_map/all_to_all | solution.py:135
  17.9 15.6 %copy-start.44 = (s32[432]{0:T(512)}, s32[432]{0:T(512)S(1)}, u32[]{:S(2)}) copy-start(s32[432]{0:T(512)S(1)} %iota_add_fusion) | copy-start | bytes 5188
  20.1 9.1 %all-to-all-start.1 = ((bf16[1,4,72,512]{3,2,0,1:T(8,128)(2,1)}), bf16[1,4,72,512]{3,2,0,1:T(8,128)(2,1)S(1)}, u32[]{:S(2)}, u32[]{:S(2)}) async-start(bf16[1,4,72,512]{3,2,0,1:T(8,128)(2,1)} %fusion.66), calls=%async_computation.1 | async-start | bytes 589824 | tf_op jit(solution)/shard_map/all_to_all | solution.py:134
  23.5 43.7 %all-gather.3.cloned.1.call-start = ((), (), s32[]{:S(2)}) async-start(), calls=%async_computation.5 | async-start | bytes 2211840 | tf_op jit(solution)/shard_map/all_gather | solution.py:152
  24.8 8.7 %copy-start.46 = (s32[288]{0:T(512)}, s32[288]{0:T(512)S(1)}, u32[]{:S(2)}) copy-start(s32[288]{0:T(512)S(1)} %eq.110) | copy-start | bytes 3460
  30.8 114.0 %copy-start.3 = (f32[432,512]{1,0:T(8,128)}, f32[432,512]{1,0:T(8,128)S(1)}, u32[]{:S(2)}) copy-start(f32[432,512]{1,0:T(8,128)S(1)} %get-tuple-element.186) | copy-start | bytes 2654212
  35.9 61.7 %all-gather.5.cloned.1.call-start = ((), (), s32[]{:S(2)}) async-start(), calls=%async_computation.6 | async-start | bytes 2211840 | tf_op jit(solution)/shard_map/all_gather | solution.py:153
  38.5 268.0 %reduce-scatter.9.cloned.1.call-start = ((), (), s32[]{:S(2)}) async-start(), calls=%async_computation.9 | async-start | bytes 2211840
  102.2 42.7 %copy-start.66 = (f32[512]{0:T(512)S(1)}, f32[512]{0:T(512)}, u32[]{:S(2)}) copy-start(f32[512]{0:T(512)} %param.36) | copy-start | bytes 6148
  146.7 7.3 %copy-start.1 = (f32[432,512]{1,0:T(8,128)}, f32[432,512]{1,0:T(8,128)S(1)}, u32[]{:S(2)}) copy-start(f32[432,512]{1,0:T(8,128)S(1)} %get-tuple-element.188) | copy-start | bytes 2654212
  146.7 7.3 %copy-start.30 = (f32[432]{0:T(512)}, f32[432]{0:T(512)S(1)}, u32[]{:S(2)}) copy-start(f32[432]{0:T(512)S(1)} %broadcast_multiply_fusion) | copy-start | bytes 5188
  279.4 56.3 %reduce-scatter.7.cloned.1.call-start = ((), (), s32[]{:S(2)}) async-start(), calls=%async_computation.8 | async-start | bytes 2211840
  292.1 157.5 %all-reduce.6.cloned.1.call-start = ((), (), s32[]{:S(2)}) async-start(), calls=%async_computation.7 | async-start | bytes 884736 | tf_op jit(solution)/shard_map/psum | solution.py:222
  303.7 37.8 %copy-start.16 = (bf16[4,4,432,32]{2,3,1,0:T(8,128)(2,1)S(1)}, bf16[4,4,432,32]{2,3,1,0:T(8,128)(2,1)}, u32[]{:S(2)}) copy-start(bf16[4,4,432,32]{2,3,1,0:T(8,128)(2,1)} %get-tuple-element.111) | copy-start | bytes 1327108
  303.7 37.8 %copy-start.41 = (f32[432]{0:T(512)S(1)}, f32[432]{0:T(512)}, u32[]{:S(2)}) copy-start(f32[432]{0:T(512)} %copy-done.40) | copy-start | bytes 5188
  303.7 37.9 %copy-start.57 = (f32[432]{0:T(512)S(1)}, f32[432]{0:T(512)}, u32[]{:S(2)}) copy-start(f32[432]{0:T(512)} %copy-done.56) | copy-start | bytes 5188
  303.7 37.9 %copy-start.61 = (f32[512]{0:T(512)S(1)}, f32[512]{0:T(512)}, u32[]{:S(2)}) copy-start(f32[512]{0:T(512)} %param.30) | copy-start | bytes 6148
  346.9 278.9 %all-reduce.8.cloned.1.call-start = ((), (), s32[]{:S(2)}) async-start(), calls=%async_computation.10 | async-start | bytes 25165824 | tf_op jit(solution)/shard_map/psum | solution.py:255
  351.6 9.2 %copy-start.17 = (bf16[1,432,512]{1,2,0:T(8,128)(2,1)S(1)}, bf16[1,432,512]{1,2,0:T(8,128)(2,1)}, u32[]{:S(2)}) copy-start(bf16[1,432,512]{1,2,0:T(8,128)(2,1)} %copy.68) | copy-start | bytes 1327108
  351.6 9.3 %copy-start.55 = (f32[432]{0:T(512)S(1)}, f32[432]{0:T(512)}, u32[]{:S(2)}) copy-start(f32[432]{0:T(512)} %copy-done.54) | copy-start | bytes 5188
  351.6 10.6 %copy-start.58 = (f32[512]{0:T(512)S(1)}, f32[512]{0:T(512)}, u32[]{:S(2)}) copy-start(f32[512]{0:T(512)} %get-tuple-element.170) | copy-start | bytes 6148
  351.7 10.6 %copy-start.59 = (f32[2048]{0:T(1024)S(1)}, f32[2048]{0:T(1024)}, u32[]{:S(2)}) copy-start(f32[2048]{0:T(1024)} %get-tuple-element.191) | copy-start | bytes 24580
  351.7 10.6 %copy-start.62 = (f32[512]{0:T(512)S(1)}, f32[512]{0:T(512)}, u32[]{:S(2)}) copy-start(f32[512]{0:T(512)} %get-tuple-element.114) | copy-start | bytes 6148
  351.7 10.6 %copy-start.63 = (f32[512]{0:T(512)S(1)}, f32[512]{0:T(512)}, u32[]{:S(2)}) copy-start(f32[512]{0:T(512)} %get-tuple-element.118) | copy-start | bytes 6148
  356.0 95.7 %copy-start.39 = (s32[4,216]{1,0:T(4,128)S(1)}, s32[4,216]{1,0:T(4,128)}, u32[]{:S(2)}) copy-start(s32[4,216]{1,0:T(4,128)} %copy-done.38) | copy-start | bytes 10372
  356.0 95.7 %copy-start.53 = (pred[4,216]{1,0:T(4,128)(4,1)S(1)}, pred[4,216]{1,0:T(4,128)(4,1)}, u32[]{:S(2)}) copy-start(pred[4,216]{1,0:T(4,128)(4,1)} %copy-done.52) | copy-start | bytes 2596
  357.3 94.4 %all-to-all-start.2 = ((bf16[1,4,72,512]{3,2,0,1:T(8,128)(2,1)}), bf16[1,4,72,512]{3,2,0,1:T(8,128)(2,1)S(1)}, u32[]{:S(2)}, u32[]{:S(2)}) async-start(bf16[1,4,72,512]{3,2,0,1:T(8,128)(2,1)} %bitcast.66), calls=%async_computation.2 | async-start | bytes 589824 | tf_op jit(solution)/shard_map/all_to_all | solution.py:230
  (67 other events, 228.1 us)
Sparse Core Ops, SparseCore 0:
  36.0 31.1 all-gather.2
  69.5 28.0 all-gather.4
  279.6 26.9 reduce-scatter.8
  309.0 26.6 reduce-scatter.6
  347.0 102.6 all-reduce.5
  456.9 168.8 all-reduce.7
where the time goes:
time: 649 us; the launch traced here: 644 us
  waiting for transfers between devices  279 us (43%)
  matrix products  146 us (22%)
  local copies, waits for them, and re-layouts  72 us (11%)
  blocking collectives  67.6 us (10%)
  other arithmetic  50.6 us (8%)
  between operations  16.2 us (2%)
  starting transfers between devices  12.4 us (2%)
    psum x1, waiting for transfers between devices, body(): lax.psum((grad_mask_token, grad_ln1_gain, grad_ln1_bias, grad_w_qkv, grad...  173 us
    psum x1, blocking collectives, body(): lax.psum((grad_mask_token, grad_ln1_gain, grad_ln1_bias, grad_w_qkv, grad...  67.6 us
    unnamed x144, local copies, waits for them, and re-layouts  51.3 us
    dot_general x4, matrix products, score_grads(): jnp.einsum('hqd,hkd->hqk', grad_mixed, values, preferred_element_type=jnp...  33.3 us
    all_gather x1, waiting for transfers between devices, body(): lax.all_gather(keys, 'band', axis=1, tiled=True)  27 us
    convert_element_type x4, other arithmetic, score_grads(): grad_scores = (attention * (grad_attention - inner)).astype(jnp.bfloat16)  26.7 us
    all_gather x1, waiting for transfers between devices, body(): lax.all_gather(values, 'band', axis=1, tiled=True)  26.6 us
    unnamed x8, waiting for transfers between devices  26.3 us
  transfers between devices with their start and end apart: 9, of which 8 were waited for; matrix products, arithmetic and copies ran while one was open for 9% of the time, Pallas kernels for 0%

commit v1 on v0

v1 whole, which is shorter than its diff:
```python
import functools

import jax
import jax.numpy as jnp
from jax import lax
from jax.experimental import pallas as pl
from jax.experimental.pallas import tpu as pltpu
from jax.sharding import Mesh, PartitionSpec as P

bf = jnp.bfloat16
f32 = jnp.float32

HEADS = 16
DEPTH = 32
QUAD = 4
GROUPS = 4
LOG2E = 1.4426950408889634
SCALE = DEPTH**-0.5
EPS = 1e-05
BIG = 1e30
PAD = 8

NT = (((1,), (1,)), ((), ()))
NN = (((1,), (0,)), ((), ()))
TN = (((0,), (0,)), ((), ()))
VMEM_LIMIT = 56 * 1024 * 1024


def dg(a, b, dims):
    return lax.dot_general(a, b, dims, preferred_element_type=f32)


def params():
    return pltpu.CompilerParams(vmem_limit_bytes=VMEM_LIMIT)


def cost(flops, nbytes, trans=0):
    return pl.CostEstimate(flops=int(flops), bytes_accessed=int(nbytes), transcendentals=int(trans))


def sds(shape, dtype):
    return jax.ShapeDtypeStruct(shape, dtype)


def prep_kernel(base_ref, v0, v1, v2, v3, ids_ref, pos_ref, mt_ref, gain_ref, bias_ref, w_ref, badd_ref, *outs, own):
    base = base_ref[pl.program_id(0)]
    rows = pos_ref.shape[-2]
    piece = v0.shape[0]
    slot = lax.broadcasted_iota(jnp.int32, (rows, piece), 0) + base
    placed = jnp.zeros((rows, pos_ref.shape[-1]), f32)
    seen = jnp.zeros((rows, 1), f32)
    for i, v in enumerate((v0, v1, v2, v3)):
        hot = (slot == ids_ref[i]).astype(f32)
        seen += jnp.sum(hot, axis=1, keepdims=True)
        placed += dg(hot.astype(bf), v[...], NN)
    pos = pos_ref[...].reshape(placed.shape).astype(f32)
    start = placed + (1.0 - seen) * mt_ref[...] + pos
    centered = start - jnp.mean(start, axis=-1, keepdims=True)
    variance = jnp.mean(centered * centered, axis=-1, keepdims=True)
    normed = (centered * lax.rsqrt(variance + EPS) * gain_ref[...] + bias_ref[...]).astype(bf)
    width = normed.shape[1]
    proj = dg(normed, w_ref[...], NN) + badd_ref[...]
    if own:
        start_ref, normed_ref, q_ref, k_ref, v_ref = outs
        start_ref[...] = start
        q_ref[...] = (proj[:, :width] * (SCALE * LOG2E)).astype(bf)
        proj = proj[:, width:]
    else:
        normed_ref, k_ref, v_ref = outs
    normed_ref[...] = normed.reshape(normed_ref.shape)
    k_ref[...] = proj[:, :width].astype(bf).reshape(k_ref.shape)
    v_ref[...] = proj[:, width:].astype(bf).reshape(v_ref.shape)


def prep(base, pieces, ids, pos, mt, gain, bias, w, badd, own):
    width = pos.shape[-1]
    rows = pos.shape[-2]
    count = 1 if own else pos.shape[0]
    full = lambda a: pl.BlockSpec(a.shape, lambda g, b: (0,) * a.ndim)
    if own:
        block = pl.BlockSpec((rows, width), lambda g, b: (0, 0))
        shape = (rows, width)
        out_shape = [sds(shape, f32)] + [sds(shape, bf)] * 4
    else:
        block = pl.BlockSpec((1, rows, width), lambda g, b: (g, 0, 0))
        shape = (count, rows, width)
        out_shape = [sds(shape, bf)] * 3
    flops = 2 * count * rows * width * (w.shape[1] + 4 * pieces[0].shape[0])
    return pl.pallas_call(
        functools.partial(prep_kernel, own=own),
        grid_spec=pltpu.PrefetchScalarGridSpec(
            num_scalar_prefetch=1,
            grid=(count,),
            in_specs=[full(p) for p in pieces] + [full(ids), block, full(mt), full(gain), full(bias), full(w), full(badd)],
            out_specs=[block] * len(out_shape),
        ),
        out_shape=out_shape,
        compiler_params=params(),
        cost_estimate=cost(flops, 4 * count * rows * width * 4),
        name="prep_own" if own else "prep_rest",
    )(base, *pieces, ids, pos, mt, gain, bias, w, badd)


def stack_heads(x):
    lane = lax.broadcasted_iota(jnp.int32, x.shape, 1) // DEPTH
    return jnp.concatenate([jnp.where(lane == h, x, jnp.zeros_like(x)) for h in range(QUAD)], axis=0)


def unstack_heads(xt):
    rows = xt.shape[1] // QUAD
    parts = [xt[DEPTH * h : DEPTH * (h + 1), rows * h : rows * (h + 1)] for h in range(QUAD)]
    return jnp.concatenate(parts, axis=0).T


def fwd_step(state, live, k, v, qs):
    m, l, o = state
    s = dg(k, qs, NT)
    top = jnp.where(live, jnp.max(s, axis=0, keepdims=True), -BIG)
    peak = jnp.maximum(m, top)
    p = jnp.exp2(s - jnp.where(live, peak, BIG))
    keep = jnp.exp2(m - peak)
    l = l * keep + jnp.sum(p, axis=0, keepdims=True)
    o = o * keep + dg(v, p.astype(bf), TN)
    return (peak, l, o)


def fwd_own_kernel(live_ref, q_ref, k_ref, v_ref, m_ref, l_ref, o_ref):
    qs = stack_heads(q_ref[...])
    n = qs.shape[0]
    live = live_ref[0] > 0
    s = dg(k_ref[...], qs, NT)
    m = jnp.where(live, jnp.max(s, axis=0, keepdims=True), -BIG)
    p = jnp.exp2(s - jnp.where(live, m, BIG))
    m_ref[0] = m
    l_ref[0] = jnp.sum(p, axis=0, keepdims=True)
    o_ref[0] = dg(v_ref[...], p.astype(bf), TN)


def fwd_rest_kernel(live_ref, q_ref, k_ref, v_ref, m_ref, l_ref, o_ref, mixed_ref, lse_ref):
    qs = stack_heads(q_ref[...])
    state = (m_ref[0], l_ref[0], o_ref[0])
    for g in range(k_ref.shape[0]):
        state = fwd_step(state, live_ref[g + 1] > 0, k_ref[g], v_ref[g], qs)
    m, l, o = state
    mixed_ref[...] = unstack_heads(o / l).astype(bf)
    lse_ref[0] = m + jnp.log2(l)


def attention_forward(live, q, k_own, v_own, k_rest, v_rest):
    rows, width = q.shape
    quads = width // 128
    n = rows * QUAD
    blk = pl.BlockSpec((rows, 128), lambda g, b: (0, g))
    vec = pl.BlockSpec((1, 1, n), lambda g, b: (g, 0, 0))
    acc = pl.BlockSpec((1, 128, n), lambda g, b: (g, 0, 0))
    rest = pl.BlockSpec((k_rest.shape[0], rows, 128), lambda g, b: (0, 0, g))
    work = 2 * rows * n * 256 * 2 * quads
    state = pl.pallas_call(
        fwd_own_kernel,
        grid_spec=pltpu.PrefetchScalarGridSpec(
            num_scalar_prefetch=1, grid=(quads,), in_specs=[blk] * 3, out_specs=[vec, vec, acc]
        ),
        out_shape=[sds((quads, 1, n), f32), sds((quads, 1, n), f32), sds((quads, 128, n), f32)],
        compiler_params=params(),
        cost_estimate=cost(work, 4 << 20, rows * n * quads),
        name="attention_own",
    )(live, q, k_own, v_own)
    return pl.pallas_call(
        fwd_rest_kernel,
        grid_spec=pltpu.PrefetchScalarGridSpec(
            num_scalar_prefetch=1,
            grid=(quads,),
            in_specs=[blk, rest, rest, vec, vec, acc],
            out_specs=[blk, vec],
        ),
        out_shape=[sds((rows, width), bf), sds((quads, 1, n), f32)],
        compiler_params=params(),
        cost_estimate=cost(3 * work, 8 << 20, 3 * rows * n * quads),
        name="attention_rest",
    )(live, q, k_rest, v_rest, *state)


def bwd_kernel(live_ref, q_ref, do_ref, k_ref, v_ref, lse_ref, delta_ref, *refs, index, last):
    *dq_in, dk_ref, dv_ref, dq_ref = refs
    qs = stack_heads(q_ref[...])
    dos = stack_heads(do_ref[...])
    k = k_ref[...].reshape(q_ref.shape)
    v = v_ref[...].reshape(q_ref.shape)
    dead = jnp.where(live_ref[index] > 0, 0.0, BIG)
    p = jnp.exp2(dg(k, qs, NT) - (lse_ref[0] + dead))
    ds = (p * (dg(v, dos, NT) - delta_ref[0])).astype(bf)
    dv_ref[...] = dg(p.astype(bf), dos, NN).astype(bf)
    dk_ref[...] = (dg(ds, qs, NN) * (1.0 / LOG2E)).astype(bf)
    dq = unstack_heads(dg(k, ds, TN))
    if dq_in:
        dq += dq_in[0][...]
    if last:
        dq_ref[...] = (dq * SCALE).astype(bf)
    else:
        dq_ref[...] = dq


def attention_backward(live, index, q, do, k, v, lse, delta, dq):
    rows, width = q.shape
    quads = width // 128
    n = rows * QUAD
    blk = pl.BlockSpec((rows, 128), lambda g, b: (0, g))
    vec = pl.BlockSpec((1, 1, n), lambda g, b: (g, 0, 0))
    if k.ndim == 3:
        kv = pl.BlockSpec((1, rows, 128), lambda g, b: (index - 1, 0, g))
    else:
        kv = blk
    last = index == 0
    extra = [] if dq is None else [dq]
    return pl.pallas_call(
        functools.partial(bwd_kernel, index=index, last=last),
        grid_spec=pltpu.PrefetchScalarGridSpec(
            num_scalar_prefetch=1,
            grid=(quads,),
            in_specs=[blk, blk, kv, kv, vec, vec] + [blk] * len(extra),
            out_specs=[blk] * 3,
        ),
        out_shape=[sds((rows, width), bf)] * 2 + [sds((rows, width), bf if last else f32)],
        compiler_params=params(),
        cost_estimate=cost(2 * rows * n * 256 * 5 * quads, 5 << 20, rows * n * quads),
        name="attention_grad_%d" % index,
    )(live, q, do, k, v, lse, delta, *extra)


def normalize(values, gain, offset):
    average = jnp.mean(values, axis=-1, keepdims=True)
    centered = values - average
    variance = jnp.mean(centered * centered, axis=-1, keepdims=True)
    return centered * lax.rsqrt(variance + EPS) * gain + offset


def smooth_gate(values):
    return jax.nn.gelu(values, approximate=True)


def column_sum(tensor):
    return jnp.sum(tensor.astype(f32), axis=0)


def shift(array, axis, step):
    size = lax.axis_size(axis)
    return lax.ppermute(array, axis, [(i, (i + step) % size) for i in range(size)])


def peers(array, axis):
    return [shift(array, axis, step) for step in (1, 3, 2)]


def swap(array):
    return shift(array, "core", 1)


def total(parts):
    return functools.reduce(jnp.add, [p.astype(f32) for p in parts])


RING = ("z", "y", "x")


def ring_scatter(array):
    chunks = 64
    rows = array.shape[0] // chunks
    got = lax.all_to_all(array.reshape(chunks, rows, array.shape[1]), RING, 0, 0, tiled=True)
    return jnp.sum(got.astype(f32), axis=0).astype(bf)


def ring_gather(chunk):
    spread = jnp.broadcast_to(chunk[None], (64,) + chunk.shape)
    got = lax.all_to_all(spread, RING, 0, 0, tiled=True)
    return got.reshape(64 * chunk.shape[0], chunk.shape[1])


def body(
    vis,
    keep_slots,
    counts,
    band_mask,
    mask_token,
    pos,
    ln1_gain,
    ln1_bias,
    w_qkv,
    b_query,
    b_value,
    w_out,
    b_out,
    ln2_gain,
    ln2_bias,
    w_up,
    b_up,
    w_down,
    b_down,
    d_out,
):
    x = lax.axis_index("x")
    core = lax.axis_index("core")
    first_core = core == 0
    piece = keep_slots.shape[1]
    rows, width = pos.shape
    half = rows // 2
    hidden = w_up.shape[1]
    d_out = d_out[0]

    index = lax.broadcasted_iota(jnp.int32, (1, piece), 1)
    code = jnp.where(index < counts, keep_slots, -1) + 1
    marks = jnp.concatenate([code // 64, code % 64], axis=0).astype(bf)
    marks = jnp.pad(marks, ((0, PAD - 2), (0, width - piece)))
    message = jnp.concatenate([vis[0], marks], axis=0)
    pieces = [message] + peers(message, "x")

    pos_half = lax.dynamic_slice(pos, (half * core, 0), (half, width))
    mine = jnp.stack(peers(pos_half, "x"))
    other = swap(mine)
    pos_rest = jnp.where(
        first_core, jnp.concatenate([mine, other], axis=1), jnp.concatenate([other, mine], axis=1)
    )

    def decode(msg):
        ids = msg[piece].astype(jnp.int32) * 64 + msg[piece + 1].astype(jnp.int32) - 1
        return ids[: piece + PAD]

    lanes = lax.broadcasted_iota(jnp.int32, (1, piece + PAD), 1)
    ids = jnp.stack([jnp.where(lanes < piece, decode(m)[None], -1) for m in pieces])

    order = (x + jnp.array([0, 3, 1, 2], jnp.int32)) % GROUPS
    base = order * rows
    live = jnp.take(band_mask[0], order)

    row = lambda a: a.reshape(1, -1)
    badd = jnp.concatenate([b_query, jnp.zeros_like(b_query), b_value])
    start, normed_own, q, k_own, v_own = prep(
        base[:1], pieces, ids, pos, row(mask_token), row(ln1_gain), row(ln1_bias), w_qkv, row(badd), True
    )
    normed_rest, k_rest, v_rest = prep(
        base[1:],
        pieces,
        ids,
        pos_rest,
        row(mask_token),
        row(ln1_gain),
        row(ln1_bias),
        w_qkv[:, width:],
        row(badd[width:]),
        False,
    )
    mixed, lse = attention_forward(live, q, k_own, v_own, k_rest, v_rest)

    branch = dg(mixed, w_out, NN) + b_out
    middle = start + branch
    normed_second = normalize(middle, ln2_gain, ln2_bias).astype(bf)
    up_value = dg(normed_second, w_up, NN) + b_up
    activated = smooth_gate(up_value).astype(bf)
    out = (middle + (dg(activated, w_down, NN) + b_down)).astype(bf)
    grad_result = d_out.astype(f32)
    grad_activated = dg(d_out, w_down, NT)
    _, gate_pull = jax.vjp(smooth_gate, up_value)
    grad_up = gate_pull(grad_activated)[0].astype(bf)
    grad_w_down = dg(activated, d_out, TN).astype(bf)
    blocks = hidden // width
    grad_w_up = jnp.concatenate(
        [dg(normed_second, grad_up[:, width * i : width * (i + 1)], TN).astype(bf) for i in range(blocks)], axis=0
    )
    grad_second = dg(grad_up, w_up, NT)
    _, second_pull = jax.vjp(normalize, middle, ln2_gain, ln2_bias)
    grad_middle_part, grad_ln2_gain, grad_ln2_bias = second_pull(grad_second)
    grad_middle = grad_result + grad_middle_part
    grad_branch = grad_middle.astype(bf)
    grad_mixed = dg(grad_branch, w_out, NT).astype(bf)
    grad_w_out = dg(mixed, grad_branch, TN).astype(bf)

    ff_kept = jnp.where(first_core, grad_w_down, grad_w_up)
    ff_sent = jnp.where(first_core, grad_w_up, grad_w_down)
    ff_half = (ff_kept.astype(f32) + swap(ff_sent).astype(f32)).astype(bf)
    ff_chunk = ring_scatter(ff_half)

    head_of = lax.broadcasted_iota(jnp.int32, (HEADS, width), 1) // DEPTH
    pick = (head_of == lax.broadcasted_iota(jnp.int32, (HEADS, width), 0)).astype(f32)
    delta = lax.dot_general(
        pick, mixed.astype(f32) * grad_mixed.astype(f32), NT, precision=lax.Precision.HIGHEST
    ).reshape(HEADS // QUAD, 1, QUAD * rows)
    w_k, w_v = w_qkv[:, width : 2 * width], w_qkv[:, 2 * width :]
    dq = None
    first_parts = []
    grad_w_k = jnp.zeros((width, width), f32)
    grad_w_v = jnp.zeros((width, width), f32)
    grad_b_value = jnp.zeros((width,), f32)
    for group, step in ((3, 2), (1, 3), (2, 1)):
        dk, dv, dq = attention_backward(live, group, q, grad_mixed, k_rest, v_rest, lse, delta, dq)
        part = (dg(dk, w_k, NT) + dg(dv, w_v, NT)).astype(bf)
        first_parts.append(shift(part, "x", step))
        grad_w_k += dg(normed_rest[group - 1], dk, TN)
        grad_w_v += dg(normed_rest[group - 1], dv, TN)
        grad_b_value += column_sum(dv)
    dk, dv, dq = attention_backward(live, 0, q, grad_mixed, k_own, v_own, lse, delta, dq)
    grad_w_k += dg(normed_own, dk, TN)
    grad_w_v += dg(normed_own, dv, TN)
    grad_b_value += column_sum(dv)
    grad_w_q = dg(normed_own, dq, TN)
    grad_b_query = column_sum(dq)

    low = jnp.concatenate([grad_w_k, grad_w_v], axis=0).astype(bf)
    high = jnp.concatenate([grad_w_q.astype(bf), grad_w_out], axis=0)
    at_kept = jnp.where(first_core, low, high)
    at_sent = jnp.where(first_core, high, low)
    at_half = (at_kept.astype(f32) + swap(at_sent).astype(f32)).astype(bf)
    at_chunk = ring_scatter(at_half)

    grad_first = dg(dq, w_qkv[:, :width], NT) + dg(dk, w_k, NT) + dg(dv, w_v, NT) + total(first_parts)
    _, first_pull = jax.vjp(normalize, start, ln1_gain, ln1_bias)
    grad_start_part, grad_ln1_gain, grad_ln1_bias = first_pull(grad_first)
    grad_start = grad_middle + grad_start_part

    slots = lax.broadcasted_iota(jnp.int32, (1, rows), 1) + base[0]
    grad_low = grad_start.astype(bf)
    shares = []
    for i in range(GROUPS):
        hot = (ids[i, 0, :piece][:, None] == slots).astype(bf)
        shares.append(dg(hot, grad_low, NN).astype(bf))
    returned = [shares[0], shift(shares[1], "x", 3), shift(shares[2], "x", 1), shift(shares[3], "x", 2)]
    grad_vis = total(returned).astype(bf)

    own_slots = lax.broadcasted_iota(jnp.int32, (rows, 1), 0) + base[0]
    seen = jnp.any(own_slots[:, :, None] == ids.reshape(1, 1, -1), axis=2)
    grad_mask_token = jnp.sum(jnp.where(seen, 0.0, grad_start), axis=0)

    vectors = jnp.stack(
        [
            grad_mask_token,
            grad_ln1_gain,
            grad_ln1_bias,
            grad_b_query,
            grad_b_value,
            column_sum(grad_branch),
            grad_ln2_gain,
            grad_ln2_bias,
            column_sum(grad_result),
        ]
    )
    vectors = jnp.concatenate([vectors, column_sum(grad_up).reshape(blocks, width)], axis=0)
    count = vectors.shape[0]
    vectors = jnp.pad(vectors, ((0, 16 - count), (0, 0))).astype(bf)
    vectors = total([vectors] + peers(vectors, "x")).astype(bf)
    upper, lower = grad_start[:half], grad_start[half:]
    pos_kept = jnp.where(first_core, upper, lower)
    pos_sent = jnp.where(first_core, lower, upper).astype(bf)
    pos_half_sum = (pos_kept + swap(pos_sent).astype(f32)).astype(bf)
    vectors = (vectors.astype(f32) + swap(vectors).astype(f32)).astype(bf)
    bundle = jnp.concatenate([pos_half_sum, vectors], axis=0)
    bundle = total([bundle] + peers(bundle, "y")).astype(bf)
    bundle = total([bundle] + peers(bundle, "z"))
    vectors = bundle[half:]
    pos_mine = bundle[:half].astype(bf)
    pos_other = swap(pos_mine)
    grad_pos = jnp.where(
        first_core, jnp.concatenate([pos_mine, pos_other]), jnp.concatenate([pos_other, pos_mine])
    ).astype(f32)

    ff_mine = ring_gather(ff_chunk)
    ff_other = swap(ff_mine)
    grad_w_down = jnp.where(first_core, ff_mine, ff_other).astype(f32)
    up_rows = jnp.where(first_core, ff_other, ff_mine).astype(f32)
    grad_w_up = up_rows.reshape(blocks, width, width).transpose(1, 0, 2).reshape(width, hidden)

    at_mine = ring_gather(at_chunk)
    at_other = swap(at_mine)
    low = jnp.where(first_core, at_mine, at_other).astype(f32)
    high = jnp.where(first_core, at_other, at_mine).astype(f32)
    grad_w_qkv = jnp.concatenate([high[:width], low[:width], low[width:]], axis=1)
    grad_w_out = high[width:]

    return (
        out[None],
        grad_vis[None],
        vectors[0],
        grad_pos,
        vectors[1],
        vectors[2],
        grad_w_qkv,
        vectors[3],
        vectors[4],
        grad_w_out,
        vectors[5],
        vectors[6],
        vectors[7],
        grad_w_up,
        vectors[9 : 9 + blocks].reshape(hidden),
        grad_w_down,
        vectors[8],
    )


CUBE = ("z", "y", "core")


def solution(mesh):
    fine = Mesh(mesh.devices.reshape(4, 4, 2, 4), ("z", "y", "core", "x"))
    return jax.shard_map(
        body,
        mesh=fine,
        in_specs=(
            P(CUBE, "x", None),
            P(CUBE, "x"),
            P(CUBE, "x"),
            P(CUBE, None),
            P(),
            P("x", None),
        )
        + (P(),) * 13
        + (P(CUBE, "x", None),),
        out_specs=(P(CUBE, "x", None), P(CUBE, "x", None), P(), P("x", None)) + (P(),) * 13,
        check_vma=False,
    )
```

time: 649 us -> 350 us (0.54)
  waiting for transfers between devices: 279 us -> 71 us
  matrix products: 146 us -> 50.3 us
  Pallas kernels: 0 us -> 84.1 us
  blocking collectives: 67.6 us -> 0 us
  starting transfers between devices: 12.4 us -> 77 us
  local copies, waits for them, and re-layouts: 72 us -> 20.8 us
  between operations: 16.2 us -> 2.78 us
  other arithmetic: 50.6 us -> 39.6 us
    psum x2 -> x0, waiting for transfers between devices: 193 us -> none  [the longest x1 173 us: body(): lax.psum((grad_mask_token, grad_ln1_gain, grad_ln1_bias, grad_w_qkv, grad...]
    dot_general x44 -> x35, matrix products: 146 us -> 50.3 us  [the longest x34 49.7 us: dg(): return lax.dot_general(a, b, dims, preferred_element_type=f32)]
    pallas_call x0 -> x8, Pallas kernels: none -> 84.1 us  [the longest x4 46.4 us: attention_backward(): pl.pallas_call(functools.partial(bwd_kernel, index=index, last=last), gri...]
    psum x1 -> x0, blocking collectives: 67.6 us -> none  [body(): lax.psum((grad_mask_token, grad_ln1_gain, grad_ln1_bias, grad_w_qkv, grad...]
    ppermute x0 -> x29, waiting for transfers between devices: none -> 63.9 us  [shift(): lax.ppermute(array, axis, [(i, (i + step) % size) for i in range(size)])]
    all_gather x2 -> x0, waiting for transfers between devices: 53.6 us -> none  [the longest x1 27 us: body(): lax.all_gather(keys, 'band', axis=1, tiled=True)]
    unnamed x144 -> x130, local copies, waits for them, and re-layouts: 51.3 us -> 3.98 us
    ppermute x0 -> x29, starting transfers between devices: none -> 42.9 us  [shift(): lax.ppermute(array, axis, [(i, (i + step) % size) for i in range(size)])]
  transfers between devices with their start and end apart: 9 -> 33, of which waited for: 8 -> 10; matrix products, arithmetic and copies ran while one was open for 9% -> 20% of each run, Pallas kernels for 0% -> 4%
where the time goes in v1:
time: 350 us; the launch traced here: 346 us
  Pallas kernels  84.1 us (24%)
  starting transfers between devices  77 us (22%)
  waiting for transfers between devices  71 us (20%)
  matrix products  50.3 us (14%)
  other arithmetic  39.6 us (11%)
  local copies, waits for them, and re-layouts  20.8 us (6%)
    ppermute x29, waiting for transfers between devices, shift(): lax.ppermute(array, axis, [(i, (i + step) % size) for i in range(size)])  63.9 us
    dot_general x34, matrix products, dg(): return lax.dot_general(a, b, dims, preferred_element_type=f32)  49.7 us
    pallas_call x4, Pallas kernels, attention_backward(): pl.pallas_call(functools.partial(bwd_kernel, index=index, last=last), gri...  46.4 us
    ppermute x29, starting transfers between devices, shift(): lax.ppermute(array, axis, [(i, (i + step) % size) for i in range(size)])  42.9 us
    pallas_call x1, Pallas kernels, attention_forward(): pl.pallas_call(fwd_rest_kernel, grid_spec=pltpu.PrefetchScalarGridSpec(nu...  17.8 us
    all_to_all x2, starting transfers between devices, ring_gather(): got = lax.all_to_all(spread, RING, 0, 0, tiled=True)  17.1 us
    all_to_all x2, starting transfers between devices, ring_scatter(): lax.all_to_all(array.reshape(chunks, rows, array.shape[1]), RING, 0, 0, t...  17 us
    pallas_call x2, Pallas kernels, prep(): pl.pallas_call(functools.partial(prep_kernel, own=own), grid_spec=pltpu.P...  12.6 us
  transfers between devices with their start and end apart: 33, of which 10 were waited for; matrix products, arithmetic and copies ran while one was open for 20% of the time, Pallas kernels for 4%

profile of v1, /device:TPU:1, one launch (start us, length us, event | category | flops | bytes accessed | tf_op | source)
XLA Modules:
  0.0 345.5 jit_solution(5364749132053145621)
XLA Ops:
  19.5 3.8 %collective-permute-done.5 = bf16[216,512]{1,0:T(8,128)(2,1)S(1)} collective-permute-done((bf16[216,512]{1,0:T(8,128)(2,1)S(1)}, bf16[216,512]{1,0:T(8,128)(2,1)S(1)}, u32[]{:S(2)}, u32[]{:S(2)}) %collective-permute-start.5) | collective-permute-done | bytes 221216 | tf_op jit(solution)/shard_map/ppermute | solution.py:247
  23.3 4.9 %collective-permute-done.3 = bf16[216,512]{1,0:T(8,128)(2,1)S(1)} collective-permute-done((bf16[216,512]{1,0:T(8,128)(2,1)S(1)}, bf16[216,512]{1,0:T(8,128)(2,1)S(1)}, u32[]{:S(2)}, u32[]{:S(2)}) %collective-permute-start.3) | collective-permute-done | bytes 221216 | tf_op jit(solution)/shard_map/ppermute | solution.py:247
  32.8 5.0 %prep_own.1 = (f32[432,512]{1,0:T(8,128)}, bf16[432,512]{1,0:T(8,128)(2,1)}, bf16[432,512]{1,0:T(8,128)(2,1)}, bf16[432,512]{1,0:T(8,128)(2,1)}, bf16[432,512]{1,0:T(8,128)(2,1)}) custom-call(s32[1]{0:T(128)} %bitcast.168, bf16[224,512]{1,0:T(8,128)(2,1)} %pad_maximum_fusion.6.v0, bf16[224,512]{1,0:T(8,128)(2,1)} %collective-permute-done.v1, ...), custom_call_target="tpu_custom_call" | custom-call | flops 1075838976 | bytes 3538944 | tf_op jit(solution)/shard_map/prep_own/pallas_call | solution.py:89
  40.6 7.3 %attention_own.1 = (f32[4,1,1728]{2,1,0:T(1,128)}, f32[4,1,1728]{2,1,0:T(1,128)}, f32[4,128,1728]{2,1,0:T(8,128)}) custom-call(s32[4]{0:T(128)} %get-tuple-element.112.live_ref, bf16[432,512]{1,0:T(8,128)(2,1)} %get-tuple-element.43.q_ref, bf16[432,512]{1,0:T(8,128)(2,1)} %get-tuple-element.46.k_ref, bf16[432,512]{1,0:T(8,128)(2,1)} %get-tuple-element.47.v_ref), custom_call_target="tpu_custom_call" | custom-call | flops 3057647616 | bytes 4194304 | tf_op jit(solution)/shard_map/attention_own/pallas_call | solution.py:158
  47.9 2.8 maximum_select_fusion.pos_ref
  50.7 7.6 %prep_rest.1 = (bf16[3,432,512]{2,1,0:T(8,128)(2,1)}, bf16[3,432,512]{2,1,0:T(8,128)(2,1)}, bf16[3,432,512]{2,1,0:T(8,128)(2,1)}) custom-call(s32[3]{0:T(128)} %slice.186.base_ref, bf16[224,512]{1,0:T(8,128)(2,1)} %pad_maximum_fusion.6.v0, bf16[224,512]{1,0:T(8,128)(2,1)} %collective-permute-done.v1, bf16[224,512]{1,0:T(8,128)(2,1)} %copy-done.59, ...), custom_call_target="tpu_custom_call" | custom-call | flops 2548039680 | bytes 10616832 | tf_op jit(solution)/shard_map/prep_rest/pallas_call | solution.py:89
  58.3 17.8 %attention_rest.1 = (bf16[432,512]{1,0:T(8,128)(2,1)}, f32[4,1,1728]{2,1,0:T(1,128)}) custom-call(s32[4]{0:T(128)} %get-tuple-element.112.live_ref, bf16[432,512]{1,0:T(8,128)(2,1)} %get-tuple-element.43.q_ref, bf16[3,432,512]{2,1,0:T(8,128)(2,1)} %get-tuple-element.44.k_ref, bf16[3,432,512]{2,1,0:T(8,128)(2,1)} %get-tuple-element.45.v_ref, ...), custom_call_target="tpu_custom_call" | custom-call | flops 9172942848 | bytes 8388608 | tf_op jit(solution)/shard_map/attention_rest/pallas_call | solution.py:168
  79.5 4.1 %fusion.124 = (bf16[2048]{0:T(1024)(128)(2,1)}, bf16[432,2048]{1,0:T(8,128)(2,1)S(1)}) fusion(f32[432,2048]{1,0:T(8,128)S(1)} %fusion.125, f32[2048]{0:T(1024)S(1)} %copy-done.60, bf16[2048,512]{1,0:T(8,128)(2,1)S(1)} %copy-done, bf16[1,432,512]{2,1,0:T(8,128)(2,1)S(1)} %copy-done.23), kind=kOutput, calls=%fused_computation.232 | convolution fusion | flops 925431808 | bytes 7860224 | tf_op jit(solution)/shard_map/dot_general | solution.py:30
  94.8 11.4 %attention_grad_3.1 = (bf16[432,512]{1,0:T(8,128)(2,1)}, bf16[432,512]{1,0:T(8,128)(2,1)}, f32[432,512]{1,0:T(8,128)}) custom-call(s32[4]{0:T(128)} %get-tuple-element.112.live_ref, bf16[432,512]{1,0:T(8,128)(2,1)} %get-tuple-element.43.q_ref, bf16[432,512]{1,0:T(8,128)(2,1)} %copy-done.35, bf16[3,432,512]{2,1,0:T(8,128)(2,1)} %get-tuple-element.44.k_ref, ...), custom_call_target="tpu_custom_call" | custom-call | flops 7644119040 | bytes 5242880 | tf_op jit(solution)/shard_map/attention_grad_3/pallas_call | solution.py:215
  106.2 11.6 %attention_grad_1.1 = (bf16[432,512]{1,0:T(8,128)(2,1)}, bf16[432,512]{1,0:T(8,128)(2,1)}, f32[432,512]{1,0:T(8,128)}) custom-call(s32[4]{0:T(128)} %get-tuple-element.112.live_ref, bf16[432,512]{1,0:T(8,128)(2,1)} %get-tuple-element.43.q_ref, bf16[432,512]{1,0:T(8,128)(2,1)} %copy-done.35, bf16[3,432,512]{2,1,0:T(8,128)(2,1)} %get-tuple-element.44.k_ref, ...), custom_call_target="tpu_custom_call" | custom-call | flops 7644119040 | bytes 5242880 | tf_op jit(solution)/shard_map/attention_grad_1/pallas_call | solution.py:215
  117.8 11.6 %attention_grad_2.1 = (bf16[432,512]{1,0:T(8,128)(2,1)}, bf16[432,512]{1,0:T(8,128)(2,1)}, f32[432,512]{1,0:T(8,128)}) custom-call(s32[4]{0:T(128)} %get-tuple-element.112.live_ref, bf16[432,512]{1,0:T(8,128)(2,1)} %get-tuple-element.43.q_ref, bf16[432,512]{1,0:T(8,128)(2,1)} %copy-done.35, bf16[3,432,512]{2,1,0:T(8,128)(2,1)} %get-tuple-element.44.k_ref, ...), custom_call_target="tpu_custom_call" | custom-call | flops 7644119040 | bytes 5242880 | tf_op jit(solution)/shard_map/attention_grad_2/pallas_call | solution.py:215
  129.4 11.9 %attention_grad_0.1 = (bf16[432,512]{1,0:T(8,128)(2,1)}, bf16[432,512]{1,0:T(8,128)(2,1)}, bf16[432,512]{1,0:T(8,128)(2,1)}) custom-call(s32[4]{0:T(128)} %get-tuple-element.112.live_ref, bf16[432,512]{1,0:T(8,128)(2,1)} %get-tuple-element.43.q_ref, bf16[432,512]{1,0:T(8,128)(2,1)} %copy-done.35, bf16[432,512]{1,0:T(8,128)(2,1)} %get-tuple-element.46.k_ref, ...), custom_call_target="tpu_custom_call" | custom-call | flops 7644119040 | bytes 5242880 | tf_op jit(solution)/shard_map/attention_grad_0/pallas_call | solution.py:215
  150.3 5.6 %broadcast_select_fusion.1 = (bf16[2048,512]{1,0:T(8,128)(2,1)}, bf16[2048,512]{1,0:T(8,128)(2,1)}) fusion(pred[]{:T(512)S(6)} %eq.87, bf16[512,512]{1,0:T(8,128)(2,1)S(1)} %copy-done.41, bf16[512,512]{1,0:T(8,128)(2,1)S(1)} %copy-done.43, bf16[512,512]{1,0:T(8,128)(2,1)S(1)} %copy-done.45, bf16[512,512]{1,0:T(8,128)(2,1)S(1)} %copy-done.47, ...), kind=kOutput, calls=%fused_computation.19 | convolution fusion | flops 925302784 | bytes 10280961 | tf_op jit(solution)/shard_map/dot_general | solution.py:30
  166.7 11.5 %all-to-all-start = ((bf16[64,16,512]{2,1,0:T(8,128)(2,1)}), bf16[64,16,512]{2,1,0:T(8,128)(2,1)}, u32[]{:S(2)}, u32[]{:S(2)}) async-start(bf16[64,16,512]{2,1,0:T(8,128)(2,1)} %bitcast.133), calls=%async_computation | async-start | bytes 2097152 | tf_op jit(solution)/shard_map/all_to_all | solution.py:268
  178.2 2.8 fusion.14
  185.8 3.0 add_convert_fusion
  188.8 7.2 %all-to-all-done = bf16[64,16,512]{2,1,0:T(8,128)(2,1)} async-done(((bf16[64,16,512]{2,1,0:T(8,128)(2,1)}), bf16[64,16,512]{2,1,0:T(8,128)(2,1)}, u32[]{:S(2)}, u32[]{:S(2)}) %all-to-all-start) | async-done | bytes 1048608 | tf_op jit(solution)/shard_map/all_to_all | solution.py:268
  196.0 5.6 %all-to-all-start.2 = ((bf16[64,32,512]{2,1,0:T(8,128)(2,1)}), bf16[64,32,512]{2,1,0:T(8,128)(2,1)}, u32[]{:S(2)}, u32[]{:S(2)}) async-start(bf16[64,32,512]{2,1,0:T(8,128)(2,1)} %bitcast.132), calls=%async_computation.2 | async-start | bytes 4194304 | tf_op jit(solution)/shard_map/all_to_all | solution.py:268
  201.6 2.7 fusion.13
  204.4 2.7 collective-permute-start.7
  210.7 23.7 %collective-permute-done.7 = bf16[432,512]{1,0:T(8,128)(2,1)} collective-permute-done((bf16[432,512]{1,0:T(8,128)(2,1)}, bf16[432,512]{1,0:T(8,128)(2,1)}, u32[]{:S(2)}, u32[]{:S(2)}) %collective-permute-start.7) | collective-permute-done | bytes 442400 | tf_op jit(solution)/shard_map/ppermute | solution.py:247
  240.3 8.5 %all-to-all-start.1 = ((bf16[64,16,512]{2,1,0:T(8,128)(2,1)}), bf16[64,16,512]{2,1,0:T(8,128)(2,1)}, u32[]{:S(2)}, u32[]{:S(2)}) async-start(bf16[64,16,512]{2,1,0:T(8,128)(2,1)} %broadcast_in_dim.90), calls=%async_computation.1 | async-start | bytes 2097152 | tf_op jit(solution)/shard_map/all_to_all | solution.py:274
  257.1 3.1 collective-permute-done.16
  260.2 6.6 %collective-permute-start.17 = (bf16[16,512]{1,0:T(8,128)(2,1)S(1)}, bf16[16,512]{1,0:T(8,128)(2,1)S(1)}, u32[]{:S(2)}, u32[]{:S(2)}) collective-permute-start(bf16[16,512]{1,0:T(8,128)(2,1)S(1)} %add_convert_fusion.7), channel_id=1, source_target_pairs={{0,4},{4,0},{1,5},{5,1},{2,6},{6,2},{3,7},{7,3},{8,12},{12,8},{9,1... | collective-permute-start | bytes 49160 | tf_op jit(solution)/shard_map/ppermute | solution.py:247
  270.3 8.6 %all-to-all-start.3 = ((bf16[64,32,512]{2,1,0:T(8,128)(2,1)}), bf16[64,32,512]{2,1,0:T(8,128)(2,1)}, u32[]{:S(2)}, u32[]{:S(2)}) async-start(bf16[64,32,512]{2,1,0:T(8,128)(2,1)} %broadcast_in_dim.91), calls=%async_computation.3 | async-start | bytes 4194304 | tf_op jit(solution)/shard_map/all_to_all | solution.py:274
  282.6 2.8 collective-permute-start.20
  287.1 22.0 %collective-permute-done.20 = bf16[232,512]{1,0:T(8,128)(2,1)S(1)} collective-permute-done((bf16[232,512]{1,0:T(8,128)(2,1)S(1)}, bf16[232,512]{1,0:T(8,128)(2,1)S(1)}, u32[]{:S(2)}, u32[]{:S(2)}) %collective-permute-start.20) | collective-permute-done | bytes 237600 | tf_op jit(solution)/shard_map/ppermute | solution.py:247
  309.2 3.2 collective-permute-start.10
  314.2 2.9 collective-permute-start.23
  324.7 3.3 collective-permute-done.22
  338.1 4.0 %select_convert_fusion = (f32[2048,512]{1,0:T(8,128)}, bf16[2048,512]{1,0:T(8,128)(2,1)S(1)}) fusion(bf16[2048,512]{1,0:T(8,128)(2,1)S(1)} %collective-permute-done.28, pred[]{:T(512)S(6)} %eq.87, bf16[64,32,512]{2,1,0:T(8,128)(2,1)} %all-to-all-done.3), kind=kLoop, calls=%fused_computation.16 | loop fusion | flops 3145728 | bytes 10485761 | tf_op jit(solution)/shard_map/convert_element_type | solution.py:465
  342.7 2.7 copy.41
  (303 shorter events, 110.7 us)
Async XLA Ops:
  3.8 27.6 %collective-permute-start = (bf16[224,512]{1,0:T(8,128)(2,1)}, bf16[224,512]{1,0:T(8,128)(2,1)}, u32[]{:S(2)}, u32[]{:S(2)}) collective-permute-start(bf16[224,512]{1,0:T(8,128)(2,1)} %pad_maximum_fusion.6.v0), channel_id=1, source_target_pairs={{0,1},{1,2},{2,3},{3,0},{4,5},{5,6},{6,7},{7,4},{8,9},{9,10},{10,1... | collective-permute-start | bytes 688136 | tf_op jit(solution)/shard_map/ppermute | solution.py:247
  5.9 24.6 %collective-permute-start.2 = (bf16[224,512]{1,0:T(8,128)(2,1)}, bf16[224,512]{1,0:T(8,128)(2,1)}, u32[]{:S(2)}, u32[]{:S(2)}) collective-permute-start(bf16[224,512]{1,0:T(8,128)(2,1)} %pad_maximum_fusion.6.v0), channel_id=1, source_target_pairs={{0,2},{1,3},{2,0},{3,1},{4,6},{5,7},{6,4},{7,5},{8,10},{9,11},{10,... | collective-permute-start | bytes 688136 | tf_op jit(solution)/shard_map/ppermute | solution.py:247
  9.3 14.0 %collective-permute-start.5 = (bf16[216,512]{1,0:T(8,128)(2,1)S(1)}, bf16[216,512]{1,0:T(8,128)(2,1)S(1)}, u32[]{:S(2)}, u32[]{:S(2)}) collective-permute-start(bf16[216,512]{1,0:T(8,128)(2,1)S(1)} %constant_dynamic-slice_fusion), channel_id=1, source_target_pairs={{0,2},{1,3},{2,0},{3,1},{4,6},{5,7},{6,4},{7,5},{8,10},{9,11},{10,... | collective-permute-start | bytes 663560 | tf_op jit(solution)/shard_map/ppermute | solution.py:247
  9.9 13.4 %collective-permute-start.4 = (bf16[216,512]{1,0:T(8,128)(2,1)S(1)}, bf16[216,512]{1,0:T(8,128)(2,1)S(1)}, u32[]{:S(2)}, u32[]{:S(2)}) collective-permute-start(bf16[216,512]{1,0:T(8,128)(2,1)S(1)} %constant_dynamic-slice_fusion), channel_id=1, source_target_pairs={{0,3},{1,0},{2,1},{3,2},{4,7},{5,4},{6,5},{7,6},{8,11},{9,8},{10,9... | collective-permute-start | bytes 663560 | tf_op jit(solution)/shard_map/ppermute | solution.py:247
  11.2 17.0 %collective-permute-start.3 = (bf16[216,512]{1,0:T(8,128)(2,1)S(1)}, bf16[216,512]{1,0:T(8,128)(2,1)S(1)}, u32[]{:S(2)}, u32[]{:S(2)}) collective-permute-start(bf16[216,512]{1,0:T(8,128)(2,1)S(1)} %constant_dynamic-slice_fusion), channel_id=1, source_target_pairs={{0,1},{1,2},{2,3},{3,0},{4,5},{5,6},{6,7},{7,4},{8,9},{9,10},{10,1... | collective-permute-start | bytes 663560 | tf_op jit(solution)/shard_map/ppermute | solution.py:247
  23.2 8.1 %collective-permute-start.1 = (bf16[224,512]{1,0:T(8,128)(2,1)}, bf16[224,512]{1,0:T(8,128)(2,1)S(1)}, u32[]{:S(2)}, u32[]{:S(2)}) collective-permute-start(bf16[224,512]{1,0:T(8,128)(2,1)} %pad_maximum_fusion.6.v0), channel_id=1, source_target_pairs={{0,3},{1,0},{2,1},{3,2},{4,7},{5,4},{6,5},{7,6},{8,11},{9,8},{10,9... | collective-permute-start | bytes 688136 | tf_op jit(solution)/shard_map/ppermute | solution.py:247
  29.1 18.9 %collective-permute-start.6 = (bf16[3,216,512]{2,1,0:T(8,128)(2,1)}, bf16[3,216,512]{2,1,0:T(8,128)(2,1)}, u32[]{:S(2)}, u32[]{:S(2)}) collective-permute-start(bf16[3,216,512]{2,1,0:T(8,128)(2,1)} %pad_maximum_fusion.4), channel_id=1, source_target_pairs={{0,4},{4,0},{1,5},{5,1},{2,6},{6,2},{3,7},{7,3},{8,12},{12,8},{9,1... | collective-permute-start | bytes 1990664 | tf_op jit(solution)/shard_map/ppermute | solution.py:247
  149.4 14.7 %collective-permute-start.25 = (bf16[1024,512]{1,0:T(8,128)(2,1)}, bf16[1024,512]{1,0:T(8,128)(2,1)}, u32[]{:S(2)}, u32[]{:S(2)}) collective-permute-start(bf16[1024,512]{1,0:T(8,128)(2,1)} %broadcast_select_fusion.2), channel_id=1, source_target_pairs={{0,4},{4,0},{1,5},{5,1},{2,6},{6,2},{3,7},{7,3},{8,12},{12,8},{9,1... | collective-permute-start | bytes 3145736 | tf_op jit(solution)/shard_map/ppermute | solution.py:247
  155.9 29.9 %collective-permute-start.27 = (bf16[2048,512]{1,0:T(8,128)(2,1)}, bf16[2048,512]{1,0:T(8,128)(2,1)}, u32[]{:S(2)}, u32[]{:S(2)}) collective-permute-start(bf16[2048,512]{1,0:T(8,128)(2,1)} %get-tuple-element.120), channel_id=1, source_target_pairs={{0,4},{4,0},{1,5},{5,1},{2,6},{6,2},{3,7},{7,3},{8,12},{12,8},{9,1... | collective-permute-start | bytes 6291464 | tf_op jit(solution)/shard_map/ppermute | solution.py:247
  162.7 48.0 %collective-permute-start.9 = (bf16[432,512]{1,0:T(8,128)(2,1)}, bf16[432,512]{1,0:T(8,128)(2,1)}, u32[]{:S(2)}, u32[]{:S(2)}) collective-permute-start(bf16[432,512]{1,0:T(8,128)(2,1)} %fusion.15), channel_id=1, source_target_pairs={{0,1},{1,2},{2,3},{3,0},{4,5},{5,6},{6,7},{7,4},{8,9},{9,10},{10,1... | collective-permute-start | bytes 1327112 | tf_op jit(solution)/shard_map/ppermute | solution.py:247
  166.7 29.3 %all-to-all-start = ((bf16[64,16,512]{2,1,0:T(8,128)(2,1)}), bf16[64,16,512]{2,1,0:T(8,128)(2,1)}, u32[]{:S(2)}, u32[]{:S(2)}) async-start(bf16[64,16,512]{2,1,0:T(8,128)(2,1)} %bitcast.133), calls=%async_computation | async-start | bytes 2097152 | tf_op jit(solution)/shard_map/all_to_all | solution.py:268
  181.1 29.6 %collective-permute-start.8 = (bf16[432,512]{1,0:T(8,128)(2,1)}, bf16[432,512]{1,0:T(8,128)(2,1)}, u32[]{:S(2)}, u32[]{:S(2)}) collective-permute-start(bf16[432,512]{1,0:T(8,128)(2,1)} %fusion.14), channel_id=1, source_target_pairs={{0,3},{1,0},{2,1},{3,2},{4,7},{5,4},{6,5},{7,6},{8,11},{9,8},{10,9... | collective-permute-start | bytes 1327112 | tf_op jit(solution)/shard_map/ppermute | solution.py:247
  196.0 43.2 %all-to-all-start.2 = ((bf16[64,32,512]{2,1,0:T(8,128)(2,1)}), bf16[64,32,512]{2,1,0:T(8,128)(2,1)}, u32[]{:S(2)}, u32[]{:S(2)}) async-start(bf16[64,32,512]{2,1,0:T(8,128)(2,1)} %bitcast.132), calls=%async_computation.2 | async-start | bytes 4194304 | tf_op jit(solution)/shard_map/all_to_all | solution.py:268
  204.4 30.0 %collective-permute-start.7 = (bf16[432,512]{1,0:T(8,128)(2,1)}, bf16[432,512]{1,0:T(8,128)(2,1)}, u32[]{:S(2)}, u32[]{:S(2)}) collective-permute-start(bf16[432,512]{1,0:T(8,128)(2,1)} %fusion.13), channel_id=1, source_target_pairs={{0,2},{1,3},{2,0},{3,1},{4,6},{5,7},{6,4},{7,5},{8,10},{9,11},{10,... | collective-permute-start | bytes 1327112 | tf_op jit(solution)/shard_map/ppermute | solution.py:247
  240.3 28.4 %all-to-all-start.1 = ((bf16[64,16,512]{2,1,0:T(8,128)(2,1)}), bf16[64,16,512]{2,1,0:T(8,128)(2,1)}, u32[]{:S(2)}, u32[]{:S(2)}) async-start(bf16[64,16,512]{2,1,0:T(8,128)(2,1)} %broadcast_in_dim.90), calls=%async_computation.1 | async-start | bytes 2097152 | tf_op jit(solution)/shard_map/all_to_all | solution.py:274
  250.7 9.5 %collective-permute-start.16 = (bf16[16,512]{1,0:T(8,128)(2,1)S(1)}, bf16[16,512]{1,0:T(8,128)(2,1)S(1)}, u32[]{:S(2)}, u32[]{:S(2)}) collective-permute-start(bf16[16,512]{1,0:T(8,128)(2,1)S(1)} %pad.11), channel_id=1, source_target_pairs={{0,2},{1,3},{2,0},{3,1},{4,6},{5,7},{6,4},{7,5},{8,10},{9,11},{10,... | collective-permute-start | bytes 49160 | tf_op jit(solution)/shard_map/ppermute | solution.py:247
  253.2 7.0 %collective-permute-start.15 = (bf16[16,512]{1,0:T(8,128)(2,1)S(1)}, bf16[16,512]{1,0:T(8,128)(2,1)S(1)}, u32[]{:S(2)}, u32[]{:S(2)}) collective-permute-start(bf16[16,512]{1,0:T(8,128)(2,1)S(1)} %pad.11), channel_id=1, source_target_pairs={{0,3},{1,0},{2,1},{3,2},{4,7},{5,4},{6,5},{7,6},{8,11},{9,8},{10,9... | collective-permute-start | bytes 49160 | tf_op jit(solution)/shard_map/ppermute | solution.py:247
  254.1 6.1 %collective-permute-start.14 = (bf16[16,512]{1,0:T(8,128)(2,1)S(1)}, bf16[16,512]{1,0:T(8,128)(2,1)S(1)}, u32[]{:S(2)}, u32[]{:S(2)}) collective-permute-start(bf16[16,512]{1,0:T(8,128)(2,1)S(1)} %pad.11), channel_id=1, source_target_pairs={{0,1},{1,2},{2,3},{3,0},{4,5},{5,6},{6,7},{7,4},{8,9},{9,10},{10,1... | collective-permute-start | bytes 49160 | tf_op jit(solution)/shard_map/ppermute | solution.py:247
  256.5 61.7 %collective-permute-start.12 = (bf16[216,512]{1,0:T(8,128)(2,1)}, bf16[216,512]{1,0:T(8,128)(2,1)}, u32[]{:S(2)}, u32[]{:S(2)}) collective-permute-start(bf16[216,512]{1,0:T(8,128)(2,1)} %convolution_convert_fusion.8), channel_id=1, source_target_pairs={{0,2},{1,3},{2,0},{3,1},{4,6},{5,7},{6,4},{7,5},{8,10},{9,11},{10,... | collective-permute-start | bytes 663560 | tf_op jit(solution)/shard_map/ppermute | solution.py:247
  260.2 20.9 %collective-permute-start.17 = (bf16[16,512]{1,0:T(8,128)(2,1)S(1)}, bf16[16,512]{1,0:T(8,128)(2,1)S(1)}, u32[]{:S(2)}, u32[]{:S(2)}) collective-permute-start(bf16[16,512]{1,0:T(8,128)(2,1)S(1)} %add_convert_fusion.7), channel_id=1, source_target_pairs={{0,4},{4,0},{1,5},{5,1},{2,6},{6,2},{3,7},{7,3},{8,12},{12,8},{9,1... | collective-permute-start | bytes 49160 | tf_op jit(solution)/shard_map/ppermute | solution.py:247
  270.3 54.4 %all-to-all-start.3 = ((bf16[64,32,512]{2,1,0:T(8,128)(2,1)}), bf16[64,32,512]{2,1,0:T(8,128)(2,1)}, u32[]{:S(2)}, u32[]{:S(2)}) async-start(bf16[64,32,512]{2,1,0:T(8,128)(2,1)} %broadcast_in_dim.91), calls=%async_computation.3 | async-start | bytes 4194304 | tf_op jit(solution)/shard_map/all_to_all | solution.py:274
  279.3 39.3 %collective-permute-start.11 = (bf16[216,512]{1,0:T(8,128)(2,1)S(1)}, bf16[216,512]{1,0:T(8,128)(2,1)S(1)}, u32[]{:S(2)}, u32[]{:S(2)}) collective-permute-start(bf16[216,512]{1,0:T(8,128)(2,1)S(1)} %convolution_convert_fusion.9), channel_id=1, source_target_pairs={{0,1},{1,2},{2,3},{3,0},{4,5},{5,6},{6,7},{7,4},{8,9},{9,10},{10,1... | collective-permute-start | bytes 663560 | tf_op jit(solution)/shard_map/ppermute | solution.py:247
  282.6 26.6 %collective-permute-start.20 = (bf16[232,512]{1,0:T(8,128)(2,1)S(1)}, bf16[232,512]{1,0:T(8,128)(2,1)S(1)}, u32[]{:S(2)}, u32[]{:S(2)}) collective-permute-start(bf16[232,512]{1,0:T(8,128)(2,1)S(1)} %pad_maximum_fusion.5), channel_id=1, source_target_pairs={{0,16},{8,24},{16,0},{24,8},{1,17},{9,25},{17,1},{25,9},{2,18},{10... | collective-permute-start | bytes 712712 | tf_op jit(solution)/shard_map/ppermute | solution.py:247
  285.3 27.3 %collective-permute-start.19 = (bf16[232,512]{1,0:T(8,128)(2,1)S(1)}, bf16[232,512]{1,0:T(8,128)(2,1)S(1)}, u32[]{:S(2)}, u32[]{:S(2)}) collective-permute-start(bf16[232,512]{1,0:T(8,128)(2,1)S(1)} %pad_maximum_fusion.5), channel_id=1, source_target_pairs={{0,24},{8,0},{16,8},{24,16},{1,25},{9,1},{17,9},{25,17},{2,26},{10... | collective-permute-start | bytes 712712 | tf_op jit(solution)/shard_map/ppermute | solution.py:247
  286.2 27.8 %collective-permute-start.18 = (bf16[232,512]{1,0:T(8,128)(2,1)S(1)}, bf16[232,512]{1,0:T(8,128)(2,1)S(1)}, u32[]{:S(2)}, u32[]{:S(2)}) collective-permute-start(bf16[232,512]{1,0:T(8,128)(2,1)S(1)} %pad_maximum_fusion.5), channel_id=1, source_target_pairs={{0,8},{8,16},{16,24},{24,0},{1,9},{9,17},{17,25},{25,1},{2,10},{10... | collective-permute-start | bytes 712712 | tf_op jit(solution)/shard_map/ppermute | solution.py:247
  309.2 13.5 %collective-permute-start.10 = (bf16[216,512]{1,0:T(8,128)(2,1)S(1)}, bf16[216,512]{1,0:T(8,128)(2,1)S(1)}, u32[]{:S(2)}, u32[]{:S(2)}) collective-permute-start(bf16[216,512]{1,0:T(8,128)(2,1)S(1)} %convolution_convert_fusion.10), channel_id=1, source_target_pairs={{0,3},{1,0},{2,1},{3,2},{4,7},{5,4},{6,5},{7,6},{8,11},{9,8},{10,9... | collective-permute-start | bytes 663560 | tf_op jit(solution)/shard_map/ppermute | solution.py:247
  314.2 10.6 %collective-permute-start.23 = (bf16[232,512]{1,0:T(8,128)(2,1)S(1)}, bf16[232,512]{1,0:T(8,128)(2,1)S(1)}, u32[]{:S(2)}, u32[]{:S(2)}) collective-permute-start(bf16[232,512]{1,0:T(8,128)(2,1)S(1)} %add_convert_fusion.3), channel_id=1, source_target_pairs={{0,64},{32,96},{64,0},{96,32},{1,65},{33,97},{65,1},{97,33},{2,66}... | collective-permute-start | bytes 712712 | tf_op jit(solution)/shard_map/ppermute | solution.py:247
  317.1 11.0 %collective-permute-start.22 = (bf16[232,512]{1,0:T(8,128)(2,1)S(1)}, bf16[232,512]{1,0:T(8,128)(2,1)S(1)}, u32[]{:S(2)}, u32[]{:S(2)}) collective-permute-start(bf16[232,512]{1,0:T(8,128)(2,1)S(1)} %add_convert_fusion.3), channel_id=1, source_target_pairs={{0,96},{32,0},{64,32},{96,64},{1,97},{33,1},{65,33},{97,65},{2,98}... | collective-permute-start | bytes 712712 | tf_op jit(solution)/shard_map/ppermute | solution.py:247
  318.1 9.9 %collective-permute-start.21 = (bf16[232,512]{1,0:T(8,128)(2,1)S(1)}, bf16[232,512]{1,0:T(8,128)(2,1)}, u32[]{:S(2)}, u32[]{:S(2)}) collective-permute-start(bf16[232,512]{1,0:T(8,128)(2,1)S(1)} %add_convert_fusion.3), channel_id=1, source_target_pairs={{0,32},{32,64},{64,96},{96,0},{1,33},{33,65},{65,97},{97,1},{2,34}... | collective-permute-start | bytes 712712 | tf_op jit(solution)/shard_map/ppermute | solution.py:247
  318.6 14.5 %collective-permute-start.26 = (bf16[1024,512]{1,0:T(8,128)(2,1)}, bf16[1024,512]{1,0:T(8,128)(2,1)}, u32[]{:S(2)}, u32[]{:S(2)}) collective-permute-start(bf16[1024,512]{1,0:T(8,128)(2,1)} %bitcast.33), channel_id=1, source_target_pairs={{0,4},{4,0},{1,5},{5,1},{2,6},{6,2},{3,7},{7,3},{8,12},{12,8},{9,1... | collective-permute-start | bytes 3145736 | tf_op jit(solution)/shard_map/ppermute | solution.py:247
  324.7 13.4 %collective-permute-start.28 = (bf16[2048,512]{1,0:T(8,128)(2,1)}, bf16[2048,512]{1,0:T(8,128)(2,1)S(1)}, u32[]{:S(2)}, u32[]{:S(2)}) collective-permute-start(bf16[2048,512]{1,0:T(8,128)(2,1)} %bitcast.40), channel_id=1, source_target_pairs={{0,4},{4,0},{1,5},{5,1},{2,6},{6,2},{3,7},{7,3},{8,12},{12,8},{9,1... | collective-permute-start | bytes 6291464 | tf_op jit(solution)/shard_map/ppermute | solution.py:247
  329.2 2.9 collective-permute-start.24
  (65 other events, 594.3 us)
